TPU v7x, 32 devices: a whole 2x2x4 slice. The times are simulated.
32 devices in a mesh: row: 4 (over y, x), col: 8 (over z, core).
Axes of the slice: x: 2, y: 2, z: 4, core: 2. Of those that a mesh axis runs over, the one named last changes fastest.
Arguments:
- tokens: bfloat16 [4096, 2880], P(('col', 'row')), may hold values from -6 to 6
- seg_ids: int32 [4096], P(('col', 'row')), may hold values from 0 to 3, never falling along the last dimension, each value on 1 to 2048 neighbouring positions
- norm_gain: float32 [2880], replicated, may hold values from 0.1 to 1.9
- query_weight: bfloat16 [2880, 4096], P('col', 'row'), may hold values from -4.5839394 to 4.5839394
- kv_weight: bfloat16 [2880, 1024], P('col', 'row'), may hold values from -0.1118034 to 0.1118034
- out_weight: bfloat16 [4096, 2880], P('row', 'col'), may hold values from -0.09375 to 0.09375
- sinks: float32 [64], P('row'), may hold values from 1 to 6
- moe_gain: float32 [2880], replicated, may hold values from 0.1 to 1.9
- routes: int32 [4096, 4], P(('col', 'row')), may hold values from 0 to 63, all different within a row; in each aligned block of 128 rows (0 to 127, 128 to 255, ...) at most 9 rows name the same one
- route_weights: float32 [4096, 4], P(('col', 'row')), may hold values from 0.05 to 0.5
- expert_in: bfloat16 [128, 2880, 1536], P(('row', 'col')), may hold values from -0.109375 to 0.109375
- expert_out: bfloat16 [128, 768, 2880], P(('row', 'col')), may hold values from -0.21875 to 0.21875
Outputs:
- mixed: bfloat16 [4096, 2880], P(('col', 'row'))
- kv_cache: bfloat16 [4096, 1024], P('col', 'row')
Inputs may be any that keep to these rules, and one draw needn't show every extreme that they name: `seg_ids`: never falling; each prompt has 1 to 2048 tokens, one exactly 2048. `routes`: each row names 4 different experts; among the 128 rows of one device no expert is named more than 9 times, and on some device one is named exactly 9 times.
All inputs are finite; a program needn't handle non-finite values.
Results may differ from a plain program's by a relative error of at most 0.012.
Values may be sent and summed in bfloat16 or wider, within the bound.
No kernel may reach another device: no remote copies, remote signals or barrier semaphores. Data moves between devices by JAX's collectives and lax.ppermute only.
A program may use at most 128 MiB of HBM per device.

v0:
```python
import math

import jax
import jax.numpy as jnp
from jax import lax
from jax.sharding import PartitionSpec as P

HD = 64
WIN = 128
EXPERTS = 64
TOP = 4
CAP = 9


eps_norm = 1e-05
theta_base = 150000.0
glu_alpha = 1.702
masked_score = -1e30


def entering(part, axis, combine, identity):
    place = lax.axis_index(axis)
    gathered = jax.tree.map(lambda a: lax.all_gather(a, axis), part)
    state = jax.tree.map(lambda a, e: jnp.zeros_like(a) + jnp.asarray(e, a.dtype), part, identity)

    def one(step, state):
        return combine(
            state, jax.tree.map(lambda a: lax.dynamic_index_in_dim(a, step, 0, False), gathered)
        )

    return lax.fori_loop(0, place, one, state)


def from_behind(value, axis, steps):
    count = lax.axis_size(axis)
    first, last = (max(0, -steps), min(count, count - steps))
    return lax.ppermute(value, axis, [(source, source + steps) for source in range(first, last)])


def rms_scale(values_in, gain_vec):
    widened = values_in.astype(jnp.float32)
    return (
        widened
        * lax.rsqrt(jnp.mean(widened * widened, axis=-1, keepdims=True) + eps_norm)
        * gain_vec
    )


def rotate(values_in, positions):
    half_dim = values_in.shape[-1] // 2
    frequency = jnp.exp(
        jnp.arange(half_dim, dtype=jnp.float32)
        * (-2.0 * math.log(theta_base) / values_in.shape[-1])
    )
    angles = positions.astype(jnp.float32)[:, None] * frequency[None, :]
    cosine = jnp.cos(angles)[:, None, :]
    sine = jnp.sin(angles)[:, None, :]
    first_half = values_in[..., :half_dim]
    second_half = values_in[..., half_dim:]
    return jnp.concatenate(
        [first_half * cosine - second_half * sine, second_half * cosine + first_half * sine],
        axis=-1,
    )


def joined(earlier, later):
    first_early, last_early, start_early = earlier
    first_late, last_late, start_late = later
    first_seg = jnp.where(first_early < 0, first_late, first_early)
    last_seg = jnp.where(last_late < 0, last_early, last_late)
    carried = (first_late == last_late) & (last_early == first_late) | (first_late < 0)
    return (first_seg, last_seg, jnp.where(carried, start_early, start_late))


def attend_tile(
    query_tile, key_tile, value_tile, query_seg, key_seg, query_pos, key_pos, sink_grid
):
    scores = jnp.einsum(
        "qkgd,lkd->kgql", query_tile, key_tile, preferred_element_type=jnp.float32
    ) * query_tile.shape[-1] ** (-0.5)
    distance = query_pos[:, None] - key_pos[None, :]
    allowed = (
        (query_seg[:, None] == key_seg[None, :])
        & (distance >= 0)
        & (distance < WIN)
        & (key_pos[None, :] >= 0)
    )
    scores = jnp.where(allowed[None, None], scores, masked_score)
    sink_col = sink_grid[:, :, None]
    ceiling = jnp.maximum(jnp.max(scores, axis=-1), sink_col)
    expo = jnp.exp(scores - ceiling[..., None])
    denom = jnp.sum(expo, axis=-1) + jnp.exp(sink_col - ceiling)
    probs = (expo / denom[..., None]).astype(jnp.bfloat16)
    return jnp.einsum(
        "kgql,lkd->qkgd", probs, value_tile, preferred_element_type=jnp.float32
    ).astype(jnp.bfloat16)


def expert_block(arrived, expert_in, expert_out):
    half_width = expert_out.shape[1]
    mixed_in = jnp.einsum("nscd,sdf->nscf", arrived, expert_in, preferred_element_type=jnp.float32)
    gate_part = mixed_in[..., :half_width]
    up_part = mixed_in[..., half_width:]
    hidden_act = (gate_part * jax.nn.sigmoid(glu_alpha * gate_part) * (up_part + 1.0)).astype(
        jnp.bfloat16
    )
    return jnp.einsum(
        "nscf,sfd->nscd", hidden_act, expert_out, preferred_element_type=jnp.float32
    ).astype(jnp.bfloat16)


def shards(
    tokens,
    seg_ids,
    norm_gain,
    query_weight,
    kv_weight,
    out_weight,
    sinks,
    moe_gain,
    routes,
    route_weights,
    expert_in,
    expert_out,
):
    feature_dim = tokens.shape[1]
    normed = rms_scale(tokens, norm_gain).astype(jnp.bfloat16)
    block_x, block_seg = (
        lax.all_gather(normed, "row", axis=0, tiled=True),
        lax.all_gather(seg_ids, "row", axis=0, tiled=True),
    )
    block_rows = block_x.shape[0]
    base_index = lax.axis_index("col") * block_rows
    token_index = base_index + jnp.arange(block_rows, dtype=jnp.int32)
    before = jnp.concatenate([block_seg[:1], block_seg[:-1]])
    own_start = lax.cummax(jnp.where(block_seg != before, token_index, base_index))
    summary = (block_seg[0], block_seg[block_rows - 1], own_start[block_rows - 1])
    neutral = (jnp.int32(-1), jnp.int32(-1), jnp.int32(-1))
    prior = entering(summary, "col", joined, neutral)
    lead_start = jnp.where(prior[1] == block_seg[0], prior[2], base_index)
    positions = token_index - jnp.where(own_start == base_index, lead_start, own_start)
    query_cols = query_weight.shape[1]
    kv_cols = kv_weight.shape[1]
    query_sum = jnp.dot(
        block_x,
        lax.all_gather(query_weight, "col", axis=0, tiled=True),
        preferred_element_type=jnp.float32,
    )
    kv_sum = jnp.dot(
        block_x,
        lax.all_gather(kv_weight, "col", axis=0, tiled=True),
        preferred_element_type=jnp.float32,
    )
    query_heads = query_cols // HD
    kv_heads = kv_cols // (2 * HD)
    group_size = query_heads // kv_heads
    queries = rotate(query_sum.reshape(block_rows, query_heads, HD), positions).astype(jnp.bfloat16)
    kv_pair = kv_sum.reshape(block_rows, kv_heads, 2, HD)
    keys = rotate(kv_pair[:, :, 0], positions).astype(jnp.bfloat16)
    values = kv_pair[:, :, 1].astype(jnp.bfloat16)
    kv_cache = jnp.stack([keys, values], axis=2).reshape(block_rows, kv_cols)
    edge_kv, edge_seg = from_behind(
        (kv_cache[block_rows - WIN :], block_seg[block_rows - WIN :]), "col", 1
    )
    all_kv = jnp.concatenate([edge_kv, kv_cache], axis=0).reshape(WIN + block_rows, kv_heads, 2, HD)
    all_seg = jnp.concatenate([edge_seg, block_seg])
    key_index = base_index - WIN + jnp.arange(WIN + block_rows, dtype=jnp.int32)
    span_rows = math.gcd(block_rows, 512)
    query_grid = queries.reshape(block_rows // span_rows, span_rows, kv_heads, group_size, HD)
    sink_grid = sinks.reshape(kv_heads, group_size)

    def attend_step(step_id):
        first_row = step_id * span_rows
        query_tile = lax.dynamic_index_in_dim(query_grid, step_id, 0, keepdims=False)
        kv_tile = lax.dynamic_slice_in_dim(all_kv, first_row, span_rows + WIN, 0)
        key_seg = lax.dynamic_slice_in_dim(all_seg, first_row, span_rows + WIN, 0)
        key_pos = lax.dynamic_slice_in_dim(key_index, first_row, span_rows + WIN, 0)
        query_seg = lax.dynamic_slice_in_dim(block_seg, first_row, span_rows, 0)
        query_pos = lax.dynamic_slice_in_dim(token_index, first_row, span_rows, 0)
        tile_out = attend_tile(
            query_tile,
            kv_tile[:, :, 0],
            kv_tile[:, :, 1],
            query_seg,
            key_seg,
            query_pos,
            key_pos,
            sink_grid,
        )
        return tile_out.reshape(span_rows, query_cols)

    attended = lax.map(attend_step, jnp.arange(block_rows // span_rows, dtype=jnp.int32)).reshape(
        block_rows, query_cols
    )
    partial_value = jnp.dot(
        attended,
        lax.all_gather(out_weight, "col", axis=1, tiled=True),
        preferred_element_type=jnp.float32,
    )
    head_total = lax.psum_scatter(
        partial_value.astype(jnp.bfloat16), "row", scatter_dimension=0, tiled=True
    ).astype(jnp.float32)
    hidden = tokens.astype(jnp.float32) + head_total
    moe_in = rms_scale(hidden, moe_gain).astype(jnp.bfloat16)
    route_flat = routes.reshape(-1)
    route_count = route_flat.shape[0]
    expert_ids = jnp.arange(EXPERTS, dtype=jnp.int32)
    hit_table = (route_flat[:, None] == expert_ids[None, :]).astype(jnp.int32)
    slot_ranks = jnp.sum((jnp.cumsum(hit_table, axis=0) - hit_table) * hit_table, axis=1)
    slot_index = route_flat * CAP + slot_ranks
    slot_table = (
        jnp.full((EXPERTS * CAP,), route_count, jnp.int32)
        .at[slot_index]
        .set(jnp.arange(route_count, dtype=jnp.int32))
    )
    padded_rows = jnp.concatenate([moe_in, jnp.zeros((1, feature_dim), jnp.bfloat16)], axis=0)
    outgoing = padded_rows[slot_table // TOP]
    outgoing = jnp.broadcast_to(
        outgoing.reshape(EXPERTS, 1, CAP, feature_dim), (EXPERTS, 2, CAP, feature_dim)
    )
    slices_here = expert_in.shape[0]
    row_count = lax.axis_size("row")
    col_count = lax.axis_size("col")
    device_count = row_count * col_count
    outgoing = outgoing.reshape(device_count, slices_here, CAP, feature_dim)
    arrived = lax.all_to_all(outgoing, ("row", "col"), split_axis=0, concat_axis=0, tiled=True)
    produced = expert_block(arrived, expert_in, expert_out)
    returned = lax.all_to_all(produced, ("row", "col"), split_axis=0, concat_axis=0, tiled=True)
    combined = jnp.sum(
        returned.reshape(EXPERTS, 2, CAP, feature_dim).astype(jnp.float32), axis=1
    ).reshape(EXPERTS * CAP, feature_dim)
    weighted = combined[slot_index] * route_weights.reshape(-1)[:, None]
    expert_total = jnp.sum(weighted.reshape(-1, TOP, feature_dim), axis=1)
    mixed = (hidden + expert_total).astype(jnp.bfloat16)
    return (mixed, kv_cache)


def solution(mesh):
    in_specs = (
        P(("col", "row"), None),
        P(("col", "row")),
        P(),
        P("col", "row"),
        P("col", "row"),
        P("row", "col"),
        P("row"),
        P(),
        P(("col", "row"), None),
        P(("col", "row"), None),
        P(("row", "col"), None, None),
        P(("row", "col"), None, None),
    )
    out_specs = (P(("col", "row"), None), P("col", "row"))
    return jax.shard_map(shards, mesh=mesh, in_specs=in_specs, out_specs=out_specs, check_vma=False)
```

profile of v0, /device:TPU:0, one launch (start us, length us, event | category | flops | bytes accessed | tf_op | source)
XLA Modules:
  0.0 775.4 jit_solution(17493078396958033960)
XLA Ops:
  12.3 9.5 %all-gather = s32[4,1,128]{2,1,0:T(1,128)S(1)} all-gather(s32[1,1,128]{2,1,0:T(1,128)} %bitcast.129), channel_id=1, replica_groups=mesh['row'=4,'col'=8] {'row'}, dimensions={0}, use_global_device_ids=true | all-gather | bytes 2560 | tf_op jit(solution)/shard_map/all_gather | solution.py:130
  27.9 9.9 %all-reduce.4 = (s32[8]{0:T(128)S(1)}, s32[8]{0:T(128)S(1)}, s32[8]{0:T(128)S(1)}) all-reduce(s32[8]{0:T(128)S(1)} %slice_dynamic-update-slice_fusion.1, s32[8]{0:T(128)S(1)} %get-tuple-element.121, s32[8]{0:T(128)S(1)} %slice_dynamic-update-slice_fusion), channel_id=1, replica_groups=mesh['row'=4,'col'=8] {'col'}, use_global_device_ids=true, to_apply=%add.1 | all-reduce | flops 24 | bytes 192
  39.0 42.3 %all-gather.6.cloned.1.call-done = bf16[512,2880]{1,0:T(8,128)(2,1)} async-done(((bf16[128,2880]{1,0:T(8,128)(2,1)}), bf16[512,2880]{1,0:T(8,128)(2,1)}) %all-gather.6.cloned.1.call-update) | async-done | bytes 2949136 | tf_op jit(solution)/shard_map/all_gather | solution.py:129
  87.5 56.9 %all-gather.10.cloned.1.call-done = bf16[2880,1024]{1,0:T(8,128)(2,1)} async-done(((bf16[360,1024]{1,0:T(8,128)(2,1)}), bf16[2880,1024]{1,0:T(8,128)(2,1)}) %all-gather.10.cloned.1.call-update) | async-done | bytes 5898256 | tf_op jit(solution)/shard_map/all_gather | solution.py:146
  165.0 41.1 %all-gather.12.cloned.1.call-done = bf16[1024,2880]{0,1:T(8,128)(2,1)} async-done(((bf16[1024,360]{0,1:T(8,128)(2,1)}), bf16[1024,2880]{0,1:T(8,128)(2,1)}) %all-gather.12.cloned.1.call-update) | async-done | bytes 5898256 | tf_op jit(solution)/shard_map/all_gather | solution.py:197
  206.1 7.3 convolution_convert_fusion
  223.3 36.4 %reduce-scatter.4.cloned.1.call-done = bf16[128,2880]{1,0:T(8,128)(2,1)} async-done(((bf16[512,2880]{1,0:T(8,128)(2,1)}), bf16[128,2880]{1,0:T(8,128)(2,1)}) %reduce-scatter.4.cloned.1.call-update) | async-done | bytes 737296 | tf_op jit(solution)/shard_map/reduce_scatter | solution.py:200
  267.2 7.2 broadcast_in_dim.75
  277.8 6.6 broadcast_in_dim.76
  284.5 15.5 %reshape.328 = bf16[32,4,9,2880]{3,1,0,2:T(4,128)(2,1)} reshape(bf16[64,2,9,2880]{3,1,0,2:T(2,128)(2,1)} %broadcast_in_dim.76) | data formatting | bytes 13271040 | tf_op jit(solution)/shard_map/reshape | solution.py:225
  300.0 8.1 %copy.97 = bf16[32,4,9,2880]{3,1,2,0:T(4,128)(2,1)} copy(bf16[32,4,9,2880]{3,1,0,2:T(4,128)(2,1)} %reshape.328) | data formatting | bytes 13271040 | tf_op jit(solution)/shard_map/reshape | solution.py:225
  308.0 155.3 %all_to_all.10 = bf16[32,4,9,2880]{3,1,2,0:T(4,128)(2,1)} all-to-all(bf16[32,4,9,2880]{3,1,2,0:T(4,128)(2,1)} %copy.97), channel_id=1, replica_groups=mesh['row'=4,'col'=8] {'row','col'}, dimensions={0} | all-to-all | bytes 13271040 | tf_op jit(solution)/shard_map/all_to_all | solution.py:226
  463.4 21.8 %fusion.10 = f32[32,4,9,1536]{3,0,2,1:T(8,128)} fusion(bf16[4,2880,1536]{2,1,0:T(8,128)(2,1)} %param.24, bf16[32,4,9,2880]{3,1,2,0:T(4,128)(2,1)} %all_to_all.10), kind=kOutput, calls=%fused_computation.17 | convolution fusion | flops 10192158720 | bytes 49102848 | tf_op jit(solution)/shard_map/nscd,sdf->nscf/dot_general | solution.py:101
  485.1 12.9 %convert_bitcast_fusion = bf16[32,4,9,2880]{3,0,2,1:T(8,128)(2,1)} fusion(bf16[4,768,2880]{1,2,0:T(8,128)(2,1)} %param.25, f32[32,4,9,1536]{3,0,2,1:T(8,128)} %fusion.10), kind=kOutput, calls=%fused_computation.15 | convolution fusion | flops 5106475008 | bytes 31408128 | tf_op jit(solution)/shard_map/nscf,sfd->nscd/dot_general | solution.py:107
  498.1 9.2 %copy.99 = bf16[32,4,9,2880]{3,1,2,0:T(4,128)(2,1)} copy(bf16[32,4,9,2880]{3,0,2,1:T(8,128)(2,1)} %convert_bitcast_fusion) | data formatting | bytes 13271040 | tf_op jit(solution)/shard_map/convert_element_type | solution.py:109
  512.3 149.5 %all-to-all-done.1 = bf16[32,4,9,2880]{3,1,2,0:T(4,128)(2,1)} async-done(((bf16[32,4,9,2880]{3,1,2,0:T(4,128)(2,1)}), bf16[32,4,9,2880]{3,1,2,0:T(4,128)(2,1)}, u32[]{:S(2)}, u32[]{:S(2)}) %all-to-all-start.1) | async-done | bytes 6635552 | tf_op jit(solution)/shard_map/all_to_all | solution.py:228
  666.4 15.5 %copy.101 = f32[32,4,9,2880]{3,1,0,2:T(4,128)} copy(f32[32,4,9,2880]{3,0,2,1:T(8,128)S(1)} %copy_convert_fusion) | data formatting | bytes 26542080 | tf_op jit(solution)/shard_map/convert_element_type | solution.py:230
  681.9 17.5 %reshape.331 = f32[64,2,9,2880]{3,1,0,2:T(2,128)} reshape(f32[32,4,9,2880]{3,1,0,2:T(4,128)} %copy.101) | data formatting | bytes 26542080 | tf_op jit(solution)/shard_map/convert_element_type | solution.py:230
  699.4 21.7 %reduce_sum.62 = f32[64,9,2880]{2,0,1:T(8,128)} reduce(f32[64,2,9,2880]{3,1,0,2:T(2,128)} %reshape.331, f32[]{:T(128)} %constant.61.clone.1), dimensions={1}, to_apply=%region_13.14 | reduce | flops 1658880 | bytes 19906564 | tf_op jit(solution)/shard_map/reduce_sum | solution.py:229
  721.1 11.6 %copy.102 = f32[64,9,2880]{2,1,0:T(8,128)} copy(f32[64,9,2880]{2,0,1:T(8,128)} %reduce_sum.62) | data formatting | bytes 13271040 | tf_op jit(solution)/shard_map/reduce_sum | solution.py:229
  732.8 9.5 %reshape.329 = f32[576,2880]{1,0:T(8,128)} reshape(f32[64,9,2880]{2,1,0:T(8,128)} %copy.102) | data formatting | bytes 13271040 | tf_op jit(solution)/shard_map/reshape | solution.py:231
  742.2 10.2 %gather_fusion.1 = f32[512,2880]{1,0:T(8,128)} fusion(f32[576,2880]{1,0:T(8,128)} %reshape.329, s32[1024]{0:T(1024)S(1)} %pad_clamp_fusion), kind=kCustom, calls=%fused_computation.1 | custom fusion | bytes 11798528 | tf_op jit(solution)/shard_map/gather | solution.py:232
  752.4 7.6 gather.10
  760.0 7.2 multiply_reduce_fusion
  (101 shorter events, 70.0 us)
Async XLA Ops:
  7.2 16.0 %copy-start.5 = (u32[32]{0:T(128)S(1)}, u32[32]{0:T(128)}, u32[]{:S(2)}) copy-start(u32[32]{0:T(128)} %constant.115) | copy-start | bytes 388
  7.2 31.6 %copy-start.4 = (f32[16]{0:T(128)S(1)}, f32[16]{0:T(128)}, u32[]{:S(2)}) copy-start(f32[16]{0:T(128)} %param.20) | copy-start | bytes 196
  7.2 31.8 %all-gather.8.cloned.1.call-start = ((), (), s32[]{:S(2)}) async-start(), calls=%async_computation.4 | async-start | bytes 1658880 | tf_op jit(solution)/shard_map/all_gather | solution.py:151
  7.9 73.3 %all-gather.6.cloned.1.call-start = ((), (), s32[]{:S(2)}) async-start(), calls=%async_computation.3 | async-start | bytes 3768320 | tf_op jit(solution)/shard_map/all_gather | solution.py:129
  11.5 132.9 %all-gather.10.cloned.1.call-start = ((), (), s32[]{:S(2)}) async-start(), calls=%async_computation.5 | async-start | bytes 6635520 | tf_op jit(solution)/shard_map/all_gather | solution.py:146
  12.3 193.9 %all-gather.12.cloned.1.call-start = ((), (), s32[]{:S(2)}) async-start(), calls=%async_computation.6 | async-start | bytes 6635520 | tf_op jit(solution)/shard_map/all_gather | solution.py:197
  21.8 17.1 %collective-permute-start.1 = (s32[128]{0:T(128)S(1)}, s32[128]{0:T(128)S(1)}, u32[]{:S(2)}, u32[]{:S(2)}) collective-permute-start(s32[128]{0:T(128)S(1)} %slice_bitcast_fusion.4), channel_id=1, source_target_pairs={{0,1},{1,2},{2,3},{3,4},{4,5},{5,6},{6,7},{8,9},{9,10},{10,11},{11... | collective-permute-start | bytes 1544 | tf_op jit(solution)/shard_map/ppermute | solution.py:37
  23.1 236.6 %reduce-scatter.4.cloned.1.call-start = ((), (), s32[]{:S(2)}) async-start(), calls=%async_computation.7 | async-start | bytes 3768320 | tf_op jit(solution)/shard_map/reduce_scatter | solution.py:200
  84.7 2.8 collective-permute-start
  213.4 4.6 copy-start.2
  213.4 47.8 %copy-start.1 = (f32[2880]{0:T(1024)S(1)}, f32[2880]{0:T(1024)}, u32[]{:S(2)}) copy-start(f32[2880]{0:T(1024)} %param.21) | copy-start | bytes 34564
  507.3 4.0 copy-start.3
  507.3 154.5 %all-to-all-start.1 = ((bf16[32,4,9,2880]{3,1,2,0:T(4,128)(2,1)}), bf16[32,4,9,2880]{3,1,2,0:T(4,128)(2,1)}, u32[]{:S(2)}, u32[]{:S(2)}) async-start(bf16[32,4,9,2880]{3,1,2,0:T(4,128)(2,1)} %copy.99), calls=%async_computation.1 | async-start | bytes 13565952 | tf_op jit(solution)/shard_map/all_to_all | solution.py:228
  760.0 7.2 copy-start
Sparse Core Ops, SparseCore 0:
  9.7 27.2 all-gather.7
  38.8 42.3 all-gather.5
  82.9 61.4 all-gather.9
  145.9 60.1 all-gather.11
  218.2 41.4 reduce-scatter.3
where the time goes:
time: 781 us; the launch traced here: 775 us
  waiting for transfers between devices  328 us (42%)
  blocking collectives  175 us (22%)
  local copies, waits for them, and re-layouts  142 us (18%)
  matrix products  60.8 us (8%)
  other arithmetic  47.5 us (6%)
  between operations  15.1 us (2%)
    all_to_all x1, blocking collectives, shards(): lax.all_to_all(outgoing, ('row', 'col'), split_axis=0, concat_axis=0, til...  155 us
    all_to_all x1, waiting for transfers between devices, shards(): lax.all_to_all(produced, ('row', 'col'), split_axis=0, concat_axis=0, til...  149 us
    all_gather x1, waiting for transfers between devices, shards(): lax.all_gather(query_weight, 'col', axis=0, tiled=True)  56.9 us
    all_gather x1, waiting for transfers between devices, shards(): lax.all_gather(normed, 'row', axis=0, tiled=True)  42.3 us
    all_gather x1, waiting for transfers between devices, shards(): lax.all_gather(out_weight, 'col', axis=1, tiled=True)  41.1 us
    reduce_scatter x1, waiting for transfers between devices, shards(): lax.psum_scatter(partial_value.astype(jnp.bfloat16), 'row', scatter_dimen...  36.4 us
    convert_element_type x2, local copies, waits for them, and re-layouts, shards(): returned.reshape(EXPERTS, 2, CAP, feature_dim).astype(jnp.float32)  33 us
    reshape x2, local copies, waits for them, and re-layouts, shards(): outgoing = outgoing.reshape(device_count, slices_here, CAP, feature_dim)  23.6 us
  transfers between devices with their start and end apart: 8, of which 5 were waited for; matrix products, arithmetic and copies ran while one was open for 5% of the time, Pallas kernels for 0%

commit v1 on v0

v1 whole, which is shorter than its diff:
```python
import math

import jax
import jax.numpy as jnp
from jax import lax
from jax.experimental import pallas as pl
from jax.experimental.pallas import tpu as pltpu
from jax.sharding import PartitionSpec as P

HD = 64
WIN = 128
EXPERTS = 64
TOP = 4
CAP = 9


eps_norm = 1e-05
theta_base = 150000.0
glu_alpha = 1.702
masked_score = -1e30


def from_behind(value, axis, steps):
    count = lax.axis_size(axis)
    first, last = (max(0, -steps), min(count, count - steps))
    return lax.ppermute(value, axis, [(source, source + steps) for source in range(first, last)])


def rms_scale(values_in, gain_vec):
    widened = values_in.astype(jnp.float32)
    return (
        widened
        * lax.rsqrt(jnp.mean(widened * widened, axis=-1, keepdims=True) + eps_norm)
        * gain_vec
    )


def rotate(values_in, positions):
    half_dim = values_in.shape[-1] // 2
    frequency = jnp.exp(
        jnp.arange(half_dim, dtype=jnp.float32)
        * (-2.0 * math.log(theta_base) / values_in.shape[-1])
    )
    angles = positions.astype(jnp.float32)[:, None] * frequency[None, :]
    cosine = jnp.cos(angles)[:, None, :]
    sine = jnp.sin(angles)[:, None, :]
    first_half = values_in[..., :half_dim]
    second_half = values_in[..., half_dim:]
    return jnp.concatenate(
        [first_half * cosine - second_half * sine, second_half * cosine + first_half * sine],
        axis=-1,
    )


def attend_tile(
    query_tile, key_tile, value_tile, query_seg, key_seg, query_pos, key_pos, sink_grid
):
    scores = jnp.einsum(
        "qkgd,lkd->kgql", query_tile, key_tile, preferred_element_type=jnp.float32
    ) * query_tile.shape[-1] ** (-0.5)
    distance = query_pos[:, None] - key_pos[None, :]
    allowed = (
        (query_seg[:, None] == key_seg[None, :])
        & (distance >= 0)
        & (distance < WIN)
        & (key_pos[None, :] >= 0)
    )
    scores = jnp.where(allowed[None, None], scores, masked_score)
    sink_col = sink_grid[:, :, None]
    ceiling = jnp.maximum(jnp.max(scores, axis=-1), sink_col)
    expo = jnp.exp(scores - ceiling[..., None])
    denom = jnp.sum(expo, axis=-1) + jnp.exp(sink_col - ceiling)
    probs = (expo / denom[..., None]).astype(jnp.bfloat16)
    return jnp.einsum(
        "kgql,lkd->qkgd", probs, value_tile, preferred_element_type=jnp.float32
    ).astype(jnp.bfloat16)


LANES = 128
MAIN = CAP - 1
FULL_VMEM = 56 * 1024 * 1024


def up_to(count, multiple):
    return -(-count // multiple) * multiple


def swap_rows(value, distance):
    count = lax.axis_size("row")
    return lax.ppermute(value, "row", [(place, place ^ distance) for place in range(count)])


def whole_spec():
    return pl.BlockSpec(memory_space=pltpu.VMEM)


def dot32(left, right):
    return jnp.dot(left, right, preferred_element_type=jnp.float32)


def piece_widths(feature_dim):
    piece = up_to(-(-feature_dim // MAIN), LANES)
    return up_to(feature_dim, LANES), piece


def as_bf16(condition):
    return jnp.where(condition, 1.0, 0.0).astype(jnp.bfloat16)


def dispatch_kernel(parts, share, feature_dim, groups, *refs):
    count = len(parts)
    tokens_ref, gain_ref = refs[:2]
    code_refs = refs[2 : 2 + groups]
    part_refs = refs[2 + groups : 2 + groups + sum(parts)]
    hidden_ref = refs[2 + groups + sum(parts)]
    out_refs = refs[3 + groups + sum(parts) : 3 + 2 * groups + sum(parts)]
    normed_ref = refs[-1]
    at = 0
    sums = []
    for index in range(count):
        total = part_refs[at][...].astype(jnp.float32)
        for other in range(1, parts[index]):
            total = total + part_refs[at + other][...].astype(jnp.float32)
        at += parts[index]
        sums.append(total)
    width = sum(share)
    pieces = []
    for block in range(feature_dim // width):
        for index in range(count):
            pieces.append(sums[index][:, block * share[index] : (block + 1) * share[index]])
    hidden = tokens_ref[...].astype(jnp.float32) + jnp.concatenate(pieces, axis=1)
    hidden_ref[...] = hidden
    scale = lax.rsqrt(jnp.mean(hidden * hidden, axis=-1, keepdims=True) + eps_norm)
    main_width, piece = piece_widths(feature_dim)
    normed_ref[...] = jnp.zeros_like(normed_ref)
    normed_ref[:, :feature_dim] = (hidden * scale * gain_ref[...]).astype(jnp.bfloat16)
    for code_ref, out_ref in zip(code_refs, out_refs):
        codes = code_ref[...]
        slot = lax.broadcasted_iota(jnp.int32, codes.shape, 0) % MAIN
        out_ref[:, :main_width] = dot32(
            as_bf16(codes == slot), normed_ref[:, :main_width]
        ).astype(jnp.bfloat16)
        tail = jnp.zeros((codes.shape[0], piece), jnp.float32)
        for j in range(MAIN):
            tail = tail + dot32(
                as_bf16((codes == MAIN) & (slot == j)), normed_ref[:, j * piece : (j + 1) * piece]
            )
        out_ref[:, main_width:] = tail.astype(jnp.bfloat16)


def dispatch(tokens, gain, codes, parts, share):
    rows, feature_dim = tokens.shape
    main_width, piece = piece_widths(feature_dim)
    flat = [part for group in parts for part in group]
    groups = len(codes)
    return pl.pallas_call(
        lambda *refs: dispatch_kernel(
            tuple(len(group) for group in parts), share, feature_dim, groups, *refs
        ),
        out_shape=[jax.ShapeDtypeStruct((rows, feature_dim), jnp.float32)]
        + [
            jax.ShapeDtypeStruct((code.shape[0], main_width + piece), jnp.bfloat16)
            for code in codes
        ],
        in_specs=[whole_spec()] * (2 + groups + len(flat)),
        out_specs=[whole_spec()] * (1 + groups),
        scratch_shapes=[pltpu.VMEM((rows, MAIN * piece), jnp.bfloat16)],
        compiler_params=pltpu.CompilerParams(vmem_limit_bytes=FULL_VMEM),
    )(tokens, gain, *codes, *flat)


def expert_kernel(feature_dim, x_ref, gate_ref, up_ref, down_ref, y_ref, x_all, total):
    main_width, piece = piece_widths(feature_dim)
    main_rows = x_ref.shape[0]
    senders = main_rows // MAIN
    step = pl.program_id(0) * pl.num_programs(1) + pl.program_id(1)
    last = pl.num_programs(0) * pl.num_programs(1) - 1

    @pl.when(step == 0)
    def _():
        x_all[:main_rows, :main_width] = x_ref[:, :main_width]
        row = lax.broadcasted_iota(jnp.int32, (senders, main_rows), 0)
        col = lax.broadcasted_iota(jnp.int32, (senders, main_rows), 1)
        tail = x_ref[:, main_width:]
        for j in range(MAIN):
            x_all[main_rows:, j * piece : (j + 1) * piece] = dot32(
                as_bf16(col == row * MAIN + j), tail
            ).astype(jnp.bfloat16)

    x = x_all[:, :feature_dim]
    gate_part = dot32(x, gate_ref[0])
    up_part = dot32(x, up_ref[0])
    hidden_act = (gate_part * jax.nn.sigmoid(glu_alpha * gate_part) * (up_part + 1.0)).astype(
        jnp.bfloat16
    )
    product = lax.dot_general(
        hidden_act, down_ref[0], (((1,), (1,)), ((), ())), preferred_element_type=jnp.float32
    )

    @pl.when(step == 0)
    def _():
        total[...] = product

    @pl.when(step > 0)
    def _():
        total[...] += product

    @pl.when(step == last)
    def _():
        y_ref[:, feature_dim:main_width] = jnp.zeros(
            (main_rows, main_width - feature_dim), jnp.bfloat16
        )
        y_ref[:, :feature_dim] = total[:main_rows].astype(jnp.bfloat16)
        x_all[main_rows:, :] = jnp.zeros((senders, MAIN * piece), jnp.bfloat16)
        x_all[main_rows:, :feature_dim] = total[main_rows:].astype(jnp.bfloat16)
        row = lax.broadcasted_iota(jnp.int32, (main_rows, senders), 0)
        col = lax.broadcasted_iota(jnp.int32, (main_rows, senders), 1)
        tail = jnp.zeros((main_rows, piece), jnp.float32)
        for j in range(MAIN):
            tail = tail + dot32(
                as_bf16(row == col * MAIN + j), x_all[main_rows:, j * piece : (j + 1) * piece]
            )
        y_ref[:, main_width:] = tail.astype(jnp.bfloat16)


def experts(x, expert_in, expert_out, first, halves):
    feature_dim, hidden_width = expert_in.shape[1], expert_out.shape[1]
    main_width, piece = piece_widths(feature_dim)
    rows = x.shape[0] + x.shape[0] // MAIN
    block = math.gcd(hidden_width, 256 if rows <= 512 else 128)
    steps = hidden_width // block
    cost = 6 * rows * feature_dim * hidden_width * halves
    return pl.pallas_call(
        lambda *refs: expert_kernel(feature_dim, *refs),
        grid=(halves, steps),
        out_shape=jax.ShapeDtypeStruct(x.shape, jnp.bfloat16),
        in_specs=[
            pl.BlockSpec(x.shape, lambda j, f: (0, 0)),
            pl.BlockSpec((1, feature_dim, block), lambda j, f: (first + j, 0, f)),
            pl.BlockSpec((1, feature_dim, block), lambda j, f: (first + j, 0, steps + f)),
            pl.BlockSpec((1, feature_dim, block), lambda j, f: (first + j, 0, f)),
        ],
        out_specs=pl.BlockSpec(x.shape, lambda j, f: (0, 0)),
        scratch_shapes=[
            pltpu.VMEM((rows, MAIN * piece), jnp.bfloat16),
            pltpu.VMEM((rows, feature_dim), jnp.float32),
        ],
        compiler_params=pltpu.CompilerParams(
            vmem_limit_bytes=FULL_VMEM, dimension_semantics=("arbitrary", "arbitrary")
        ),
        cost_estimate=pl.CostEstimate(
            flops=cost,
            bytes_accessed=6 * feature_dim * hidden_width * halves,
            transcendentals=rows * hidden_width * halves,
        ),
    )(x, expert_in, expert_in, jnp.swapaxes(expert_out, 1, 2))


def combine_kernel(turned, hidden_ref, back_ref, code_ref, weight_ref, out_ref):
    feature_dim = hidden_ref.shape[1]
    main_width, piece = piece_widths(feature_dim)
    codes = code_ref[...]
    slot = lax.broadcasted_iota(jnp.int32, codes.shape, 1) % MAIN
    weights = weight_ref[...]
    high = weights.astype(jnp.bfloat16).astype(jnp.float32)
    low = weights - high

    def pick(condition):
        return [
            jnp.where(condition, part, 0.0).astype(jnp.bfloat16) for part in (high, low)
        ]

    tail = back_ref[:, main_width:]
    main = pick(codes == slot)
    for j in range(MAIN):
        first, end = j * piece, min((j + 1) * piece, feature_dim)
        ninth = pick((codes == MAIN) & (slot == j))
        value = hidden_ref[:, first:end]
        for k in range(2):
            value = value + dot32(main[k], back_ref[:, first:end])
            value = value + dot32(ninth[k], tail)[:, : end - first]
        if turned:
            out_ref[first:end, :] = value.T.astype(out_ref.dtype)
        else:
            out_ref[:, first:end] = value


def combine(hidden, back, codes, weights, turned):
    rows, feature_dim = hidden.shape
    return pl.pallas_call(
        lambda *refs: combine_kernel(turned, *refs),
        out_shape=jax.ShapeDtypeStruct((feature_dim, rows), jnp.bfloat16)
        if turned
        else jax.ShapeDtypeStruct((rows, feature_dim), jnp.float32),
        in_specs=[whole_spec()] * 4,
        out_specs=whole_spec(),
        compiler_params=pltpu.CompilerParams(vmem_limit_bytes=FULL_VMEM),
    )(hidden, back, codes, weights)


def shards(
    tokens,
    seg_ids,
    norm_gain,
    query_weight,
    kv_weight,
    out_weight,
    sinks,
    moe_gain,
    routes,
    route_weights,
    expert_in,
    expert_out,
):
    own_rows, feature_dim = tokens.shape
    row_count, col_count = lax.axis_size("row"), lax.axis_size("col")
    device_count = row_count * col_count
    row_at, col_at = lax.axis_index("row"), lax.axis_index("col")
    query_cols, kv_cols = query_weight.shape[1], kv_weight.shape[1]

    proj_weight = lax.all_gather(
        jnp.concatenate([query_weight, kv_weight], axis=1), "col", axis=0, tiled=True
    )
    out_cols = out_weight.shape[1]
    cut = up_to(2 * out_cols // 3, 8)
    out_parts = [
        lax.all_gather(part, "col", axis=1, tiled=True)
        for part in (out_weight[:, :cut], out_weight[:, cut:])
    ]

    normed = rms_scale(tokens, norm_gain).astype(jnp.bfloat16)
    block_x = jnp.zeros((row_count, own_rows, feature_dim), jnp.bfloat16)
    for distance in range(row_count):
        piece = swap_rows(normed, distance) if distance else normed
        block_x = lax.dynamic_update_index_in_dim(block_x, piece, row_at ^ distance, 0)
    block_rows = row_count * own_rows
    block_x = block_x.reshape(block_rows, feature_dim)

    all_segs = lax.all_to_all(
        jnp.broadcast_to(seg_ids[None, :], (device_count, own_rows)),
        ("col", "row"),
        split_axis=0,
        concat_axis=0,
        tiled=True,
    ).reshape(-1)
    base_index = col_at * block_rows
    padded_segs = jnp.concatenate([jnp.full((WIN,), -1, jnp.int32), all_segs])
    key_seg = lax.dynamic_slice_in_dim(padded_segs, base_index, WIN + block_rows, 0)
    block_seg = key_seg[WIN:]
    token_index = base_index + jnp.arange(block_rows, dtype=jnp.int32)
    starts = jnp.sum((all_segs[None, :] < block_seg[:, None]).astype(jnp.int32), axis=1)
    positions = token_index - starts

    slices_here = expert_in.shape[0]
    groups = max(1, slices_here // 2)
    halves = min(2, slices_here)
    expert_ids = jnp.arange(EXPERTS, dtype=jnp.int32)
    named = routes[:, :, None] == expert_ids[None, None, :]
    hits = jnp.sum(named.astype(jnp.float32), axis=1)
    expert_weight = jnp.sum(jnp.where(named, route_weights[:, :, None], 0.0), axis=1)
    ranks = jnp.cumsum(hits, axis=0) - hits
    ranks = jnp.where(hits > 0, ranks, -1.0).astype(jnp.int32)
    code_in, code_out, weight_out = [], [], []
    for group in range(groups):
        chosen = jnp.arange(device_count, dtype=jnp.int32) * slices_here // 2 + group
        spread = jnp.repeat(ranks[:, chosen], MAIN, axis=1)
        code_out.append(spread)
        code_in.append(spread.T)
        weight_out.append(jnp.repeat(expert_weight[:, chosen], MAIN, axis=1))

    proj_sum = dot32(block_x, proj_weight)
    query_sum, kv_sum = proj_sum[:, :query_cols], proj_sum[:, query_cols:]
    query_heads = query_cols // HD
    kv_heads = kv_cols // (2 * HD)
    group_size = query_heads // kv_heads
    queries = rotate(query_sum.reshape(block_rows, query_heads, HD), positions).astype(jnp.bfloat16)
    kv_pair = kv_sum.reshape(block_rows, kv_heads, 2, HD)
    keys = rotate(kv_pair[:, :, 0], positions).astype(jnp.bfloat16)
    values = kv_pair[:, :, 1].astype(jnp.bfloat16)
    kv_cache = jnp.stack([keys, values], axis=2).reshape(block_rows, kv_cols)
    edge_kv = from_behind(kv_cache[block_rows - WIN :], "col", 1)
    all_kv = jnp.concatenate([edge_kv, kv_cache], axis=0).reshape(WIN + block_rows, kv_heads, 2, HD)
    key_index = base_index - WIN + jnp.arange(WIN + block_rows, dtype=jnp.int32)
    query_grid = queries.reshape(block_rows, kv_heads, group_size, HD)
    sink_grid = sinks.reshape(kv_heads, group_size)
    attended = attend_tile(
        query_grid,
        all_kv[:, :, 0],
        all_kv[:, :, 1],
        block_seg,
        key_seg,
        token_index,
        key_index,
        sink_grid,
    ).reshape(block_rows, query_cols)

    sums = []
    for part in out_parts:
        if sums:
            part, sums = lax.optimization_barrier((part, sums))
        partial = dot32(attended, part).astype(jnp.bfloat16)
        partial = partial.reshape(row_count, own_rows, part.shape[1])
        pieces = []
        for distance in range(row_count):
            piece = lax.dynamic_index_in_dim(partial, row_at ^ distance, 0, False)
            pieces.append(swap_rows(piece, distance) if distance else piece)
        sums.append(pieces)

    hidden, *outgoing = dispatch(
        tokens, moe_gain.reshape(1, feature_dim), code_in, sums, (cut, out_cols - cut)
    )
    for group in range(groups):
        shape = (device_count, MAIN, outgoing[group].shape[1])
        arrived = lax.all_to_all(
            outgoing[group].reshape(shape), ("row", "col"), split_axis=0, concat_axis=0, tiled=True
        )
        produced = experts(
            arrived.reshape(outgoing[group].shape), expert_in, expert_out, group * halves, halves
        )
        returned = lax.all_to_all(
            produced.reshape(shape), ("row", "col"), split_axis=0, concat_axis=0, tiled=True
        )
        hidden = combine(
            hidden,
            returned.reshape(outgoing[group].shape),
            code_out[group],
            weight_out[group],
            group == groups - 1,
        )
    return (hidden.T, kv_cache)


def solution(mesh):
    in_specs = (
        P(("col", "row"), None),
        P(("col", "row")),
        P(),
        P("col", "row"),
        P("col", "row"),
        P("row", "col"),
        P("row"),
        P(),
        P(("col", "row"), None),
        P(("col", "row"), None),
        P(("row", "col"), None, None),
        P(("row", "col"), None, None),
    )
    out_specs = (P(("col", "row"), None), P("col", "row"))
    return jax.shard_map(shards, mesh=mesh, in_specs=in_specs, out_specs=out_specs, check_vma=False)
```

time: 781 us -> 380 us (0.49)
  waiting for transfers between devices: 328 us -> 164 us
  blocking collectives: 175 us -> 45 us
  local copies, waits for them, and re-layouts: 142 us -> 36.5 us
  Pallas kernels: 0 us -> 50.3 us
  matrix products: 60.8 us -> 24.8 us
  other arithmetic: 47.5 us -> 15.2 us
  starting transfers between devices: 7.49 us -> 29.8 us
    all_to_all x1, blocking collectives: 155 us -> 45 us  [shards(): lax.all_to_all(outgoing[group].reshape(shape), ('row', 'col'), split_axis...]
    all_gather x4 -> x3, waiting for transfers between devices: 140 us -> 55.5 us  [the longest x2 27.8 us: shards(): lax.all_gather(part, 'col', axis=1, tiled=True)]
    all_to_all x1 -> x4, waiting for transfers between devices: 149 us -> 99.1 us  [the longest x2 55.7 us: shards(): lax.all_to_all(produced.reshape(shape), ('row', 'col'), split_axis=0, con...]
    pallas_call x0 -> x5, Pallas kernels: none -> 50.3 us  [the longest x2 36.2 us: experts(): pl.pallas_call(lambda *refs: expert_kernel(feature_dim, *refs), grid=(hal...]
    convert_element_type x3 -> x0, local copies, waits for them, and re-layouts: 42.2 us -> none  [the longest x2 33 us: shards(): returned.reshape(EXPERTS, 2, CAP, feature_dim).astype(jnp.float32)]
    reduce_scatter x1 -> x0, waiting for transfers between devices: 36.4 us -> none  [shards(): lax.psum_scatter(partial_value.astype(jnp.bfloat16), 'row', scatter_dimen...]
    dot_general x5 -> x3, matrix products: 51.8 us -> 15.7 us  [dot32(): return jnp.dot(left, right, preferred_element_type=jnp.float32)]
    reduce_sum x3 -> x2, other arithmetic: 29 us -> 1.04 us  [the longest x1 1.01 us: shards(): jnp.sum((all_segs[None, :] < block_seg[:, None]).astype(jnp.int32), axis=1)]
  transfers between devices with their start and end apart: 8 -> 17, of which waited for: 5 -> 10; matrix products, arithmetic and copies ran while one was open for 5% -> 17% of each run, Pallas kernels for 0% -> 11%
where the time goes in v1:
time: 380 us; the launch traced here: 379 us
  waiting for transfers between devices  164 us (43%)
  Pallas kernels  50.3 us (13%)
  blocking collectives  45 us (12%)
  local copies, waits for them, and re-layouts  36.5 us (10%)
  starting transfers between devices  29.8 us (8%)
  matrix products  24.8 us (7%)
  other arithmetic  15.2 us (4%)
  between operations  14.2 us (4%)
    all_to_all x2, waiting for transfers between devices, shards(): lax.all_to_all(produced.reshape(shape), ('row', 'col'), split_axis=0, con...  55.7 us
    all_to_all x1, blocking collectives, shards(): lax.all_to_all(outgoing[group].reshape(shape), ('row', 'col'), split_axis...  45 us
    pallas_call x2, Pallas kernels, experts(): pl.pallas_call(lambda *refs: expert_kernel(feature_dim, *refs), grid=(hal...  36.2 us
    all_gather x2, waiting for transfers between devices, shards(): lax.all_gather(part, 'col', axis=1, tiled=True)  27.8 us
    all_gather x1, waiting for transfers between devices, shards(): lax.all_gather(jnp.concatenate([query_weight, kv_weight], axis=1), 'col',...  27.7 us
    all_to_all x1, waiting for transfers between devices, shards(): lax.all_to_all(outgoing[group].reshape(shape), ('row', 'col'), split_axis...  23.6 us
    all_to_all x1, waiting for transfers between devices, shards(): lax.all_to_all(jnp.broadcast_to(seg_ids[None, :], (device_count, own_rows...  19.8 us
    dot_general x3, matrix products, dot32(): return jnp.dot(left, right, preferred_element_type=jnp.float32)  15.7 us
  transfers between devices with their start and end apart: 17, of which 10 were waited for; matrix products, arithmetic and copies ran while one was open for 17% of the time, Pallas kernels for 11%

profile of v1, /device:TPU:0, one launch (start us, length us, event | category | flops | bytes accessed | tf_op | source)
XLA Modules:
  0.0 379.5 jit_solution(8619995724858751808)
XLA Ops:
  11.4 3.0 collective-permute-start
  16.5 6.3 %all-to-all-start = ((s32[32,1,128]{2,1,0:T(1,128)}), s32[32,1,128]{2,1,0:T(1,128)S(1)}, u32[]{:S(2)}, u32[]{:S(2)}) async-start(s32[32,1,128]{2,1,0:T(1,128)} %broadcast_in_dim.97), calls=%async_computation | async-start | bytes 32768 | tf_op jit(solution)/shard_map/all_to_all | solution.py:339
  28.6 19.8 %all-to-all-done = s32[32,1,128]{2,1,0:T(1,128)S(1)} async-done(((s32[32,1,128]{2,1,0:T(1,128)}), s32[32,1,128]{2,1,0:T(1,128)S(1)}, u32[]{:S(2)}, u32[]{:S(2)}) %all-to-all-start) | async-done | bytes 16416 | tf_op jit(solution)/shard_map/all_to_all | solution.py:339
  58.6 27.7 %all-gather.6.cloned.1.call-done = bf16[2880,1280]{1,0:T(8,128)(2,1)} async-done(((bf16[360,1280]{1,0:T(8,128)(2,1)}), bf16[2880,1280]{1,0:T(8,128)(2,1)}) %all-gather.6.cloned.1.call-update) | async-done | bytes 7372816 | tf_op jit(solution)/shard_map/all_gather | solution.py:321
  86.4 8.2 %fusion.21 = f32[512,1280]{1,0:T(8,128)S(1)} fusion(bf16[512,2880]{1,0:T(8,128)(2,1)} %bitcast.12, bf16[2880,1280]{1,0:T(8,128)(2,1)} %all-gather.6.cloned.1.call-done), kind=kOutput, calls=%fused_computation.87 | convolution fusion | flops 3774873600 | bytes 12943360 | tf_op jit(solution)/shard_map/dot_general | solution.py:98
  101.1 2.8 collective-permute-start.3
  108.7 3.2 fusion.1
  112.0 4.5 %fusion = f32[2,8,512]{2,1,0:T(8,128)S(1)} fusion(f32[2,640,512,8]{2,1,3,0:T(8,128)S(1)} %get-tuple-element.45, f32[2,8,512]{2,1,0:T(8,128)S(1)} %broadcast_maximum_fusion, pred[512,640]{0,1:T(8,128)(4,1)S(1)} %fusion.9), kind=kLoop, calls=%fused_computation.7 | loop fusion | flops 20963328 | bytes 21364736 | tf_op jit(solution)/shard_map/reduce_sum | solution.py:72
  116.6 5.9 %fusion.3 = bf16[2,64,8,512]{3,1,2,0:T(8,128)(2,1)S(1)} fusion(f32[2,640,512,8]{2,1,3,0:T(8,128)S(1)} %get-tuple-element.45, f32[2,8,512]{2,1,0:T(8,128)S(1)} %exponential_add_fusion, f32[2,8,512]{2,1,0:T(8,128)S(1)} %broadcast_maximum_fusion, pred[512,640]{0,1:T(8,128)(4,1)S(1)} %fusion.9, bf16[640,2,2,64]{0,3,1,2:T(8,128)(2,1)S(1)} %maximum_maximum_fusion), kind=kOutput, calls=%fused_computation.16 | convolution fusion | flops 697827328 | bytes 22577152 | tf_op jit(solution)/shard_map/kgql,lkd->qkgd/dot_general | solution.py:74
  122.5 8.8 %all-gather.8.cloned.1.call-done = bf16[1024,1920]{0,1:T(8,128)(2,1)} async-done(((bf16[1024,240]{0,1:T(8,128)(2,1)}), bf16[1024,1920]{0,1:T(8,128)(2,1)}) %all-gather.8.cloned.1.call-update) | async-done | bytes 3932176 | tf_op jit(solution)/shard_map/all_gather | solution.py:327
  131.4 4.5 %convolution_convert_fusion = bf16[512,1920]{1,0:T(8,128)(2,1)S(1)} fusion(bf16[512,1024]{0,1:T(8,128)(2,1)S(1)} %bitcast.129, bf16[1024,1920]{0,1:T(8,128)(2,1)} %all-gather.8.cloned.1.call-done), kind=kOutput, calls=%fused_computation.11 | convolution fusion | flops 2014248960 | bytes 6946816 | tf_op jit(solution)/shard_map/dot_general | solution.py:98
  142.2 19.0 %all-gather.4.cloned.1.call-done = bf16[1024,960]{0,1:T(8,128)(2,1)} async-done(((bf16[1024,120]{0,1:T(8,128)(2,1)}), bf16[1024,960]{0,1:T(8,128)(2,1)}) %all-gather.4.cloned.1.call-update) | async-done | bytes 1966096 | tf_op jit(solution)/shard_map/all_gather | solution.py:327
  163.3 3.0 convolution_convert_fusion.1
  177.1 4.9 %collective-permute-done.8.refs_10_ = bf16[128,960]{1,0:T(8,128)(2,1)S(1)} collective-permute-done((bf16[128,960]{1,0:T(8,128)(2,1)S(1)}, bf16[128,960]{1,0:T(8,128)(2,1)S(1)}, u32[]{:S(2)}, u32[]{:S(2)}) %collective-permute-start.8) | collective-permute-done | bytes 245792 | tf_op jit(solution)/shard_map/ppermute | solution.py:90
  182.9 5.8 %shard_map.131 = (f32[128,2880]{1,0:T(8,128)}, bf16[256,3328]{1,0:T(8,128)(2,1)}, bf16[256,3328]{1,0:T(8,128)(2,1)}) custom-call(bf16[128,2880]{1,0:T(8,128)(2,1)} %copy.106.refs_0_, f32[1,2880]{1,0:T(1,128)} %reshape.353.refs_1_, s32[256,128]{1,0:T(8,128)} %get-tuple-element.41.refs_2_, s32[256,128]{1,0:T(8,128)} %get-tuple-element.39.refs_3_, ...), custom_call_target="tpu_custom_call" | custom-call | tf_op jit(solution)/shard_map/pallas_call | solution.py:156
  188.8 45.0 %all_to_all.26 = bf16[32,8,3328]{2,1,0:T(8,128)(2,1)} all-to-all(bf16[32,8,3328]{2,1,0:T(8,128)(2,1)} %bitcast.120), channel_id=1, replica_groups=mesh['row'=4,'col'=8] {'row','col'}, dimensions={0} | all-to-all | bytes 3407872 | tf_op jit(solution)/shard_map/all_to_all | solution.py:414
  236.5 18.1 %shard_map.132 = bf16[256,3328]{1,0:T(8,128)(2,1)} custom-call(bf16[256,3328]{1,0:T(8,128)(2,1)} %bitcast.111, bf16[4,2880,1536]{2,1,0:T(8,128)(2,1)} %refs_2_.3, bf16[4,2880,1536]{2,1,0:T(8,128)(2,1)} %refs_2_.3, bf16[4,2880,768]{2,1,0:T(8,128)(2,1)} %bitcast.104), custom_call_target="tpu_custom_call" | custom-call | flops 7644119040 | bytes 26542080 | tf_op jit(solution)/shard_map/pallas_call | solution.py:233
  254.6 23.6 %all-to-all-done.3 = bf16[32,8,3328]{2,1,0:T(8,128)(2,1)S(1)} async-done(((bf16[32,8,3328]{2,1,0:T(8,128)(2,1)}), bf16[32,8,3328]{2,1,0:T(8,128)(2,1)S(1)}, u32[]{:S(2)}, u32[]{:S(2)}) %all-to-all-start.3) | async-done | bytes 1703968 | tf_op jit(solution)/shard_map/all_to_all | solution.py:414
  282.1 18.1 %shard_map.134 = bf16[256,3328]{1,0:T(8,128)(2,1)} custom-call(bf16[256,3328]{1,0:T(8,128)(2,1)} %bitcast.109, bf16[4,2880,1536]{2,1,0:T(8,128)(2,1)} %refs_2_.3, bf16[4,2880,1536]{2,1,0:T(8,128)(2,1)} %refs_2_.3, bf16[4,2880,768]{2,1,0:T(8,128)(2,1)} %bitcast.105), custom_call_target="tpu_custom_call" | custom-call | flops 7644119040 | bytes 26542080 | tf_op jit(solution)/shard_map/pallas_call | solution.py:233
  300.2 23.6 %all-to-all-done.2 = bf16[32,8,3328]{2,1,0:T(8,128)(2,1)S(1)} async-done(((bf16[32,8,3328]{2,1,0:T(8,128)(2,1)}), bf16[32,8,3328]{2,1,0:T(8,128)(2,1)S(1)}, u32[]{:S(2)}, u32[]{:S(2)}) %all-to-all-start.2) | async-done | bytes 1703968 | tf_op jit(solution)/shard_map/all_to_all | solution.py:420
  323.8 3.7 all-to-all-start.4
  332.5 4.2 %shard_map.133.refs_0_ = f32[128,2880]{1,0:T(8,128)} custom-call(f32[128,2880]{1,0:T(8,128)} %get-tuple-element.15.refs_0_, bf16[256,3328]{1,0:T(8,128)(2,1)} %bitcast.107, s32[128,256]{1,0:T(8,128)} %copy.107.refs_2_, f32[128,256]{1,0:T(8,128)} %copy.108.refs_3_), custom_call_target="tpu_custom_call" | custom-call | tf_op jit(solution)/shard_map/pallas_call | solution.py:290
  336.8 32.1 %all-to-all-done.4 = bf16[32,8,3328]{2,1,0:T(8,128)(2,1)} async-done(((bf16[32,8,3328]{2,1,0:T(8,128)(2,1)}), bf16[32,8,3328]{2,1,0:T(8,128)(2,1)}, u32[]{:S(2)}, u32[]{:S(2)}) %all-to-all-start.4) | async-done | bytes 1703968 | tf_op jit(solution)/shard_map/all_to_all | solution.py:420
  368.9 4.0 %shard_map.135 = bf16[2880,128]{1,0:T(8,128)(2,1)} custom-call(f32[128,2880]{1,0:T(8,128)} %shard_map.133.refs_0_, bf16[256,3328]{1,0:T(8,128)(2,1)} %bitcast.52.refs_1_, s32[128,256]{1,0:T(8,128)} %copy.109.refs_2_, f32[128,256]{1,0:T(8,128)} %copy.110.refs_3_), custom_call_target="tpu_custom_call" | custom-call | tf_op jit(solution)/shard_map/pallas_call | solution.py:290
  (145 shorter events, 65.2 us)
Async XLA Ops:
  7.2 8.7 %copy-start.21 = (s32[128]{0:T(128)S(1)}, s32[128]{0:T(128)}, u32[]{:S(2)}) copy-start(s32[128]{0:T(128)} %param.13) | copy-start | bytes 1540
  7.2 79.2 %all-gather.6.cloned.1.call-start = ((), (), s32[]{:S(2)}) async-start(), calls=%async_computation.6 | async-start | bytes 8294400 | tf_op jit(solution)/shard_map/all_gather | solution.py:321
  9.6 121.8 %all-gather.8.cloned.1.call-start = ((), (), s32[]{:S(2)}) async-start(), calls=%async_computation.7 | async-start | bytes 4423680 | tf_op jit(solution)/shard_map/all_gather | solution.py:327
  10.5 14.6 %copy-start.19 = (f32[128,4]{0,1:T(4,128)S(1)}, f32[128,4]{0,1:T(4,128)}, u32[]{:S(2)}) copy-start(f32[128,4]{0,1:T(4,128)} %param.21) | copy-start | bytes 6148
  10.5 14.6 %copy-start.20 = (s32[128,4]{0,1:T(4,128)S(1)}, s32[128,4]{0,1:T(4,128)}, u32[]{:S(2)}) copy-start(s32[128,4]{0,1:T(4,128)} %param.20) | copy-start | bytes 6148
  11.4 39.2 %collective-permute-start = (bf16[128,2880]{0,1:T(8,128)(2,1)S(1)}, bf16[128,2880]{0,1:T(8,128)(2,1)}, u32[]{:S(2)}, u32[]{:S(2)}) collective-permute-start(bf16[128,2880]{0,1:T(8,128)(2,1)S(1)} %fusion.6), channel_id=1, source_target_pairs={{0,8},{8,0},{16,24},{24,16},{1,9},{9,1},{17,25},{25,17},{2,10},{10... | collective-permute-start | bytes 2211848 | tf_op jit(solution)/shard_map/ppermute | solution.py:90
  14.4 37.7 %collective-permute-start.1 = (bf16[128,2880]{0,1:T(8,128)(2,1)S(1)}, bf16[128,2880]{0,1:T(8,128)(2,1)}, u32[]{:S(2)}, u32[]{:S(2)}) collective-permute-start(bf16[128,2880]{0,1:T(8,128)(2,1)S(1)} %fusion.6), channel_id=1, source_target_pairs={{0,16},{8,24},{16,0},{24,8},{1,17},{9,25},{17,1},{25,9},{2,18},{10... | collective-permute-start | bytes 2211848 | tf_op jit(solution)/shard_map/ppermute | solution.py:90
  15.9 37.6 %collective-permute-start.2 = (bf16[128,2880]{0,1:T(8,128)(2,1)S(1)}, bf16[128,2880]{0,1:T(8,128)(2,1)}, u32[]{:S(2)}, u32[]{:S(2)}) collective-permute-start(bf16[128,2880]{0,1:T(8,128)(2,1)S(1)} %fusion.6), channel_id=1, source_target_pairs={{0,24},{8,16},{16,8},{24,0},{1,25},{9,17},{17,9},{25,1},{2,26},{10... | collective-permute-start | bytes 2211848 | tf_op jit(solution)/shard_map/ppermute | solution.py:90
  16.5 31.9 %all-to-all-start = ((s32[32,1,128]{2,1,0:T(1,128)}), s32[32,1,128]{2,1,0:T(1,128)S(1)}, u32[]{:S(2)}, u32[]{:S(2)}) async-start(s32[32,1,128]{2,1,0:T(1,128)} %broadcast_in_dim.97), calls=%async_computation | async-start | bytes 32768 | tf_op jit(solution)/shard_map/all_to_all | solution.py:339
  22.8 138.3 %all-gather.4.cloned.1.call-start = ((), (), s32[]{:S(2)}) async-start(), calls=%async_computation.5 | async-start | bytes 2211840 | tf_op jit(solution)/shard_map/all_gather | solution.py:327
  49.8 48.9 %copy-start.5 = (f32[512,32]{0,1:T(8,128)}, f32[512,32]{0,1:T(8,128)S(1)}, u32[]{:S(2)}) copy-start(f32[512,32]{0,1:T(8,128)S(1)} %get-tuple-element.43) | copy-start | bytes 196612
  101.1 6.6 %collective-permute-start.3 = (bf16[128,256]{0,1:T(8,128)(2,1)}, bf16[128,256]{0,1:T(8,128)(2,1)}, u32[]{:S(2)}, u32[]{:S(2)}) collective-permute-start(bf16[128,256]{0,1:T(8,128)(2,1)} %bitcast.18), channel_id=1, source_target_pairs={{0,1},{1,2},{2,3},{3,4},{4,5},{5,6},{6,7},{8,9},{9,10},{10,11},{11... | collective-permute-start | bytes 196616 | tf_op jit(solution)/shard_map/ppermute | solution.py:26
  122.5 13.4 %copy-start.25 = (bf16[2,64,8,512]{3,1,2,0:T(8,128)(2,1)}, bf16[2,64,8,512]{3,1,2,0:T(8,128)(2,1)S(1)}, u32[]{:S(2)}) copy-start(bf16[2,64,8,512]{3,1,2,0:T(8,128)(2,1)S(1)} %fusion.3) | copy-start | bytes 3145732
  137.1 24.1 %collective-permute-start.4 = (bf16[128,1920]{1,0:T(8,128)(2,1)}, bf16[128,1920]{1,0:T(8,128)(2,1)S(1)}, u32[]{:S(2)}, u32[]{:S(2)}) collective-permute-start(bf16[128,1920]{1,0:T(8,128)(2,1)} %get-tuple-element.30), channel_id=1, source_target_pairs={{0,8},{8,0},{16,24},{24,16},{1,9},{9,1},{17,25},{25,17},{2,10},{10... | collective-permute-start | bytes 1474568 | tf_op jit(solution)/shard_map/ppermute | solution.py:90
  138.5 23.8 %collective-permute-start.5 = (bf16[128,1920]{1,0:T(8,128)(2,1)}, bf16[128,1920]{1,0:T(8,128)(2,1)S(1)}, u32[]{:S(2)}, u32[]{:S(2)}) collective-permute-start(bf16[128,1920]{1,0:T(8,128)(2,1)} %get-tuple-element.29), channel_id=1, source_target_pairs={{0,16},{8,24},{16,0},{24,8},{1,17},{9,25},{17,1},{25,9},{2,18},{10... | collective-permute-start | bytes 1474568 | tf_op jit(solution)/shard_map/ppermute | solution.py:90
  140.0 22.4 %collective-permute-start.6 = (bf16[128,1920]{1,0:T(8,128)(2,1)S(1)}, bf16[128,1920]{1,0:T(8,128)(2,1)S(1)}, u32[]{:S(2)}, u32[]{:S(2)}) collective-permute-start(bf16[128,1920]{1,0:T(8,128)(2,1)S(1)} %get-tuple-element.28), channel_id=1, source_target_pairs={{0,24},{8,16},{16,8},{24,0},{1,25},{9,17},{17,9},{25,1},{2,26},{10... | collective-permute-start | bytes 1474568 | tf_op jit(solution)/shard_map/ppermute | solution.py:90
  166.3 6.8 %copy-start.17 = (f32[2880]{0:T(1024)S(1)}, f32[2880]{0:T(1024)}, u32[]{:S(2)}) copy-start(f32[2880]{0:T(1024)} %param.19) | copy-start | bytes 34564
  167.9 9.2 %collective-permute-start.7 = (bf16[128,960]{1,0:T(8,128)(2,1)S(1)}, bf16[128,960]{1,0:T(8,128)(2,1)S(1)}, u32[]{:S(2)}, u32[]{:S(2)}) collective-permute-start(bf16[128,960]{1,0:T(8,128)(2,1)S(1)} %get-tuple-element.34), channel_id=1, source_target_pairs={{0,8},{8,0},{16,24},{24,16},{1,9},{9,1},{17,25},{25,17},{2,10},{10... | collective-permute-start | bytes 737288 | tf_op jit(solution)/shard_map/ppermute | solution.py:90
  169.0 13.1 %collective-permute-start.8 = (bf16[128,960]{1,0:T(8,128)(2,1)S(1)}, bf16[128,960]{1,0:T(8,128)(2,1)S(1)}, u32[]{:S(2)}, u32[]{:S(2)}) collective-permute-start(bf16[128,960]{1,0:T(8,128)(2,1)S(1)} %get-tuple-element.33), channel_id=1, source_target_pairs={{0,16},{8,24},{16,0},{24,8},{1,17},{9,25},{17,1},{25,9},{2,18},{10... | collective-permute-start | bytes 737288 | tf_op jit(solution)/shard_map/ppermute | solution.py:90
  169.9 12.2 %collective-permute-start.9 = (bf16[128,960]{1,0:T(8,128)(2,1)S(1)}, bf16[128,960]{1,0:T(8,128)(2,1)S(1)}, u32[]{:S(2)}, u32[]{:S(2)}) collective-permute-start(bf16[128,960]{1,0:T(8,128)(2,1)S(1)} %get-tuple-element.32), channel_id=1, source_target_pairs={{0,24},{8,16},{16,8},{24,0},{1,25},{9,17},{17,9},{25,1},{2,26},{10... | collective-permute-start | bytes 737288 | tf_op jit(solution)/shard_map/ppermute | solution.py:90
  233.8 44.4 %all-to-all-start.3 = ((bf16[32,8,3328]{2,1,0:T(8,128)(2,1)}), bf16[32,8,3328]{2,1,0:T(8,128)(2,1)S(1)}, u32[]{:S(2)}, u32[]{:S(2)}) async-start(bf16[32,8,3328]{2,1,0:T(8,128)(2,1)} %bitcast.119), calls=%async_computation.3 | async-start | bytes 3407872 | tf_op jit(solution)/shard_map/all_to_all | solution.py:414
  279.4 44.4 %all-to-all-start.2 = ((bf16[32,8,3328]{2,1,0:T(8,128)(2,1)}), bf16[32,8,3328]{2,1,0:T(8,128)(2,1)S(1)}, u32[]{:S(2)}, u32[]{:S(2)}) async-start(bf16[32,8,3328]{2,1,0:T(8,128)(2,1)} %bitcast.110), calls=%async_computation.2 | async-start | bytes 3407872 | tf_op jit(solution)/shard_map/all_to_all | solution.py:420
  323.8 7.9 %copy-start.1 = (bf16[32,8,3328]{2,1,0:T(8,128)(2,1)}, bf16[32,8,3328]{2,1,0:T(8,128)(2,1)S(1)}, u32[]{:S(2)}) copy-start(bf16[32,8,3328]{2,1,0:T(8,128)(2,1)S(1)} %all-to-all-done.2) | copy-start | bytes 5111812
  323.8 45.1 %all-to-all-start.4 = ((bf16[32,8,3328]{2,1,0:T(8,128)(2,1)}), bf16[32,8,3328]{2,1,0:T(8,128)(2,1)}, u32[]{:S(2)}, u32[]{:S(2)}) async-start(bf16[32,8,3328]{2,1,0:T(8,128)(2,1)} %bitcast.108), calls=%async_computation.4 | async-start | bytes 3407872 | tf_op jit(solution)/shard_map/all_to_all | solution.py:420
  (19 other events, 45.2 us)
Sparse Core Ops, SparseCore 0:
  9.7 76.6 all-gather.5
  88.0 43.3 all-gather.7
  133.6 27.4 all-gather.3
